TPU v7x, 32 devices: a whole 2x2x4 slice. The times are simulated.
32 devices in a mesh: group: 2 (over y), seq: 8 (over z, x), head: 2 (over core).
Axes of the slice: x: 2, y: 2, z: 4, core: 2. Of those that a mesh axis runs over, the one named last changes fastest.
Arguments:
- x_stream: bfloat16 [2048, 4096], P(('group', 'seq'), 'head'), parts along dimension 0, may hold values from -6 to 6
- z_stream: bfloat16 [2048, 4096], P(('group', 'seq'), 'head'), parts along dimension 0, may hold values from -6 to 6
- b_stream: bfloat16 [2048, 1024], P(('group', 'seq'), 'head'), parts along dimension 0, may hold values from -6 to 6
- c_stream: bfloat16 [2048, 1024], P(('group', 'seq'), 'head'), parts along dimension 0, may hold values from -6 to 6
- dt_raw: float32 [128, 2048], P('head', ('group', 'seq')), parts along dimension 1, may hold values from -6 to 4
- a_log: float32 [256], P(('group', 'head')), parts along dimension 0, may hold values from -10 to 0
- skip_coef: float32 [128], P('head'), may hold values from 0.5 to 2
- conv_x: float32 [4, 4096], P(None, 'head'), may hold values from -3 to 3
- conv_b: float32 [4, 1024], P(None, 'head'), may hold values from -3 to 3
- conv_c: float32 [4, 1024], P(None, 'head'), may hold values from -3 to 3
- norm_gain: float32 [4096], P('head'), may hold values from 0.1 to 1.9
- state_in: float32 [256, 32, 128], P(('group', 'head')), parts along dimension 0, may hold values from -6 to 6
- grad_out: bfloat16 [2048, 4096], P(('group', 'seq'), 'head'), parts along dimension 0, may hold values from -6 to 6
Outputs:
- grad_x: bfloat16 [2048, 4096], P(('group', 'seq'), 'head'), parts along dimension 0
- grad_z: bfloat16 [2048, 4096], P(('group', 'seq'), 'head'), parts along dimension 0
- grad_b: bfloat16 [2048, 1024], P(('group', 'seq'), 'head'), parts along dimension 0
- grad_c: bfloat16 [2048, 1024], P(('group', 'seq'), 'head'), parts along dimension 0
- grad_dt: float32 [128, 2048], P('head', ('group', 'seq')), parts along dimension 1
There are 2 independent parts, one for each index of `group`. A program takes and returns all parts, laid end to end along the dimension named above; an argument that names none is the same for every part. Nothing has to cross between parts.
All inputs are finite; a program needn't handle non-finite values.
Results may differ from a plain program's by a relative error of at most 0.001.
Values may be sent and summed in bfloat16 or wider, within the bound.
A program may use at most 128 MiB of HBM per device.

v0:
```python
import jax
import jax.numpy as jnp
from jax import lax
from jax.sharding import PartitionSpec as P

EPS = 1e-05
EXACT = lax.Precision.HIGHEST


def from_behind(array, axis, by):
    peers = lax.axis_size(axis)
    pairs = [(i, i + by) for i in range(peers) if 0 <= i + by < peers]
    return lax.ppermute(array, axis, pairs)


def prefix_2(value, axis, join, neutral, backward):
    count, mine = (lax.axis_size(axis), lax.axis_index(axis))
    pieces = jax.tree.map(lambda part: lax.all_gather(part, axis), value)
    if backward:
        pieces = jax.tree.map(lambda part: part[::-1], pieces)
        mine = count - 1 - mine
    subtotal = jax.tree.map(
        lambda part, zero: jnp.full_like(part, 0) + jnp.asarray(zero, part.dtype), value, neutral
    )

    def hop(position, subtotal):
        longer = join(subtotal, jax.tree.map(lambda part: part[position], pieces))
        return jax.tree.map(lambda new, old: jnp.where(position < mine, new, old), longer, subtotal)

    return lax.fori_loop(0, count - 1, hop, subtotal)


def causal_conv(edge_rows, values, weight):
    width = weight.shape[0]
    length = values.shape[0]
    joined = jnp.concatenate([edge_rows.astype(jnp.float32), values.astype(jnp.float32)], axis=0)
    summed = jnp.zeros((length, values.shape[1]), jnp.float32)
    for offset in range(width):
        summed = summed + weight[offset][None, :] * joined[offset : offset + length]
    return summed


def conv_transpose(grad_pre, weight):
    width = weight.shape[0]
    length = grad_pre.shape[0]
    padded = jnp.pad(grad_pre, ((width - 1, width - 1), (0, 0)))
    summed = jnp.zeros((length + width - 1, grad_pre.shape[1]), jnp.float32)
    for offset in range(width):
        begin = width - 1 - offset
        summed = summed + weight[offset][None, :] * padded[begin : begin + length + width - 1]
    return summed


def activate(pre_x, pre_b, pre_c, dt_raw, a_log):
    signal = jax.nn.silu(pre_x)
    b_coef = jax.nn.silu(pre_b)
    c_coef = jax.nn.silu(pre_c)
    steps = jax.nn.softplus(dt_raw)
    rates = -jnp.exp(a_log)[:, None] * steps
    cumulative = jnp.cumsum(rates, axis=1)
    return (signal, b_coef, c_coef, steps, cumulative)


def block_summary(signal, b_coef, steps, cumulative, group_count):
    length = signal.shape[0]
    head_count = steps.shape[0]
    per_group = head_count // group_count
    head_dim = signal.shape[1] // head_count
    state_width = b_coef.shape[1] // group_count
    weights = jnp.exp(cumulative[:, -1:] - cumulative) * steps
    scaled = (
        signal.reshape(length, group_count, per_group, head_dim)
        * weights.T.reshape(length, group_count, per_group)[..., None]
    )
    b_groups = b_coef.reshape(length, group_count, state_width)
    summary = jnp.einsum("tgjp,tgn->gjpn", scaled, b_groups, precision=EXACT)
    return (jnp.exp(cumulative[:, -1]), summary.reshape(head_count, head_dim, state_width))


def block_output(
    signal,
    b_coef,
    c_coef,
    steps,
    cumulative,
    entering,
    gate_rows,
    skip_coef,
    norm_gain,
    group_count,
):
    length = signal.shape[0]
    head_count = steps.shape[0]
    per_group = head_count // group_count
    head_dim = signal.shape[1] // head_count
    state_width = b_coef.shape[1] // group_count
    b_groups = b_coef.reshape(length, group_count, state_width)
    c_groups = c_coef.reshape(length, group_count, state_width)
    scores = jnp.einsum("tgn,rgn->gtr", c_groups, b_groups, precision=EXACT)
    causal = jnp.arange(length)[:, None] >= jnp.arange(length)[None, :]
    log_gaps = cumulative[:, :, None] - cumulative[:, None, :]
    mask_decay = jnp.exp(jnp.where(causal[None], log_gaps, -jnp.inf)).reshape(
        group_count, per_group, length, length
    )
    mixing = scores[:, None] * mask_decay
    inputs_x = signal.reshape(length, group_count, per_group, head_dim)
    scaled = inputs_x * steps.T.reshape(length, group_count, per_group)[..., None]
    within = jnp.einsum("gjtr,rgjp->tgjp", mixing, scaled, precision=EXACT)
    carried = jnp.einsum(
        "tgn,gjpn->tgjp",
        c_groups,
        entering.reshape(group_count, per_group, head_dim, state_width),
        precision=EXACT,
    )
    carried = carried * jnp.exp(cumulative).T.reshape(length, group_count, per_group)[..., None]
    mixed = (
        within + carried + skip_coef.reshape(group_count, per_group)[None, :, :, None] * inputs_x
    )
    gated = mixed * jax.nn.silu(gate_rows.reshape(length, group_count, per_group, head_dim))
    inv_rms = lax.rsqrt(jnp.mean(gated * gated, axis=(2, 3), keepdims=True) + EPS)
    return (gated * inv_rms).reshape(length, head_count * head_dim) * norm_gain[None, :]


def combine_pairs(earlier, later):
    return (earlier[0] * later[0], later[0][:, None, None] * earlier[1] + later[1])


def per_device(
    x_stream,
    z_stream,
    b_stream,
    c_stream,
    dt_raw,
    a_log,
    skip_coef,
    conv_x,
    conv_b,
    conv_c,
    norm_gain,
    state_in,
    grad_out,
):
    width = conv_x.shape[0]
    edge = width - 1
    group_count = b_stream.shape[1] // state_in.shape[2]
    edge_x, edge_b, edge_c = from_behind(
        (x_stream[-edge:], b_stream[-edge:], c_stream[-edge:]), "seq", 1
    )
    pre_x = causal_conv(edge_x, x_stream, conv_x)
    pre_b = causal_conv(edge_b, b_stream, conv_b)
    pre_c = causal_conv(edge_c, c_stream, conv_c)

    def activate_local(first, second, third, fourth):
        return activate(first, second, third, fourth, a_log)

    acts, activate_back = jax.vjp(activate_local, pre_x, pre_b, pre_c, dt_raw)
    signal, b_coef, c_coef, steps, cumulative = acts

    def summary_local(first, second, third, fourth):
        return block_summary(first, second, third, fourth, group_count)

    (decay, summary), summary_back = jax.vjp(summary_local, signal, b_coef, steps, cumulative)
    identity = (jnp.ones_like(decay), jnp.zeros_like(summary))
    prefix = prefix_2((decay, summary), "seq", combine_pairs, identity, False)
    entering = prefix[1] + prefix[0][:, None, None] * state_in
    gate_rows = z_stream.astype(jnp.float32)

    def output_local(first, second, third, fourth, fifth, sixth, seventh):
        return block_output(
            first, second, third, fourth, fifth, sixth, seventh, skip_coef, norm_gain, group_count
        )

    normed, output_back = jax.vjp(
        output_local, signal, b_coef, c_coef, steps, cumulative, entering, gate_rows
    )
    d_signal, d_bcoef, d_ccoef, d_steps, d_cumul, d_enter, d_gate = output_back(
        grad_out.astype(jnp.float32)
    )
    suffix = prefix_2((decay, d_enter), "seq", combine_pairs, identity, True)
    d_exit = suffix[1]
    d_decay = jnp.sum(d_exit * entering, axis=(1, 2))
    s_signal, s_bcoef, s_steps, s_cumul = summary_back((d_decay, d_exit))
    g_prex, g_preb, g_prec, g_raw = activate_back(
        (d_signal + s_signal, d_bcoef + s_bcoef, d_ccoef, d_steps + s_steps, d_cumul + s_cumul)
    )
    full_x = conv_transpose(g_prex, conv_x)
    full_b = conv_transpose(g_preb, conv_b)
    full_c = conv_transpose(g_prec, conv_c)
    back_x, back_b, back_c = from_behind((full_x[:edge], full_b[:edge], full_c[:edge]), "seq", -1)
    own_x = full_x[edge:].at[-edge:].add(back_x)
    own_b = full_b[edge:].at[-edge:].add(back_b)
    own_c = full_c[edge:].at[-edge:].add(back_c)
    return (
        own_x.astype(jnp.bfloat16),
        d_gate.astype(jnp.bfloat16),
        own_b.astype(jnp.bfloat16),
        own_c.astype(jnp.bfloat16),
        g_raw,
    )


def solution(mesh):
    return jax.shard_map(
        per_device,
        mesh=mesh,
        in_specs=(
            P(("group", "seq"), "head"),
            P(("group", "seq"), "head"),
            P(("group", "seq"), "head"),
            P(("group", "seq"), "head"),
            P("head", ("group", "seq")),
            P(("group", "head")),
            P("head"),
            P(None, "head"),
            P(None, "head"),
            P(None, "head"),
            P("head"),
            P(("group", "head"), None, None),
            P(("group", "seq"), "head"),
        ),
        out_specs=(
            P(("group", "seq"), "head"),
            P(("group", "seq"), "head"),
            P(("group", "seq"), "head"),
            P(("group", "seq"), "head"),
            P("head", ("group", "seq")),
        ),
        check_vma=False,
    )
```

profile of v0, /device:TPU:0, one launch (start us, length us, event | category | flops | bytes accessed | tf_op | source)
XLA Modules:
  0.0 370.8 jit_solution(3350083032242749200)
XLA Ops:
  8.0 4.8 %collective-permute-start = (bf16[3,2048]{1,0:T(4,128)(2,1)S(1)}, bf16[3,2048]{1,0:T(4,128)(2,1)S(1)}, u32[]{:S(2)}, u32[]{:S(2)}) collective-permute-start(bf16[3,2048]{1,0:T(4,128)(2,1)S(1)} %slice.203), channel_id=1, source_target_pairs={{0,2},{2,4},{4,6},{6,8},{8,10},{10,12},{12,14},{1,3},{3,5},{5,7},{... | collective-permute-start | bytes 36872 | tf_op jit(solution)/shard_map/ppermute | solution.py:13
  13.5 3.4 collective-permute-start.2
  21.7 1.1 convert_element_type.44
  24.9 1.6 fusion.52
  26.9 2.0 fusion.56
  29.6 4.0 %collective-permute-start.1 = (bf16[3,512]{1,0:T(4,128)(2,1)}, bf16[3,512]{1,0:T(4,128)(2,1)}, u32[]{:S(2)}, u32[]{:S(2)}) collective-permute-start(bf16[3,512]{1,0:T(4,128)(2,1)} %slice.211), channel_id=1, source_target_pairs={{0,2},{2,4},{4,6},{6,8},{8,10},{10,12},{12,14},{1,3},{3,5},{5,7},{... | collective-permute-start | bytes 9224 | tf_op jit(solution)/shard_map/ppermute | solution.py:13
  34.2 1.2 convert_multiply_fusion
  38.2 18.8 %all-reduce.5 = f32[512]{0:T(512)S(1)} all-reduce(f32[512]{0:T(512)S(1)} %dynamic-update-slice.9), channel_id=2, replica_groups=mesh['group'=2,'seq'=8,'head'=2] {'seq'}, use_global_device_ids=true, to_apply=%add.5 | all-reduce | flops 512 | bytes 4096
  57.7 1.6 copy.58
  59.2 2.3 copy.64
  61.6 1.3 mul.539
  64.4 2.4 fusion.88
  66.9 1.7 reshape.235
  68.6 1.8 copy.69
  70.4 2.3 fusion.117
  72.7 82.3 %all-gather.4.cloned.1.call-done = f32[8,64,32,128]{3,2,1,0:T(8,128)} async-done(((f32[1,64,32,128]{3,2,1,0:T(8,128)}), f32[8,64,32,128]{3,2,1,0:T(8,128)}) %all-gather.4.cloned.1.call-update) | async-done | bytes 8388624 | tf_op jit(solution)/shard_map/all_gather | solution.py:18
  155.0 19.2 %while.33 = (s32[]{:T(128)}, f32[64]{0:T(128)}, f32[64,32,128]{2,1,0:T(8,128)S(1)}, s32[]{:T(128)}, f32[8,64]{1,0:T(8,128)}, /*index=5*/f32[8,64,32,128]{3,2,1,0:T(8,128)}, s32[]{:T(128)}, s32[]{:T(128)}) while((s32[]{:T(128)}, f32[64]{0:T(128)}, f32[64,32,128]{2,1,0:T(8,128)S(1)}, s32[]{:T(128)}, f32[8,64]{1,0:T(8,128)}, ...), condition=%wide.region_2.3_spmd.clone, body=%wide.region_1.2_spmd.clone.sunk | while | flops 1048772 | bytes 3147123 | solution.py:30
  155.0 1.2 broadcast_select_fusion.3
  156.2 1.5 fusion.130
  157.7 1.2 broadcast_select_fusion.3
  158.9 1.5 fusion.130
  160.4 1.2 broadcast_select_fusion.3
  161.6 1.5 fusion.130
  163.1 1.2 broadcast_select_fusion.3
  164.3 1.5 fusion.130
  165.8 1.2 broadcast_select_fusion.3
  167.0 1.5 fusion.130
  168.5 1.2 broadcast_select_fusion.3
  169.8 1.5 fusion.130
  171.3 1.2 broadcast_select_fusion.3
  172.5 1.5 fusion.130
  174.2 1.5 multiply_add_fusion.2
  176.7 2.0 convolution_bitcast_fusion.1
  178.7 6.8 %multiply_reduce_fusion.6 = (f32[128,4]{0,1:T(4,128)S(1)}, f32[128,4]{0,1:T(4,128)S(1)}, f32[128,4,16,32]{0,3,2,1:T(8,128)S(1)}) fusion(f32[128,2048]{0,1:T(8,128)S(1)} %copy-done.2, f32[128,2048]{0,1:T(8,128)S(1)} %copy.58, f32[128,4,16,32]{0,3,2,1:T(8,128)S(1)} %bitcast.155, f32[4,16]{1,0:T(4,128)S(1)} %copy-done.27, ...), kind=kOutput, calls=%fused_computation.71 | convolution fusion | flops 409467904 | bytes 5624064 | tf_op jit(solution)/shard_map/jvp(gjtr,rgjp->tgjp)/dot_general | solution.py:108
  185.6 2.2 multiply_reduce_fusion.2
  187.8 2.1 fusion.46
  189.9 1.3 rev.6
  191.2 3.1 convolution_bitcast_fusion.3
  194.3 10.9 %fusion.8 = (f32[4,16,128]{2,1,0:T(8,128)S(1)}, f32[4,16,128]{2,1,0:T(8,128)}, f32[4,128,128]{2,1,0:T(8,128)S(1)}) fusion(f32[4,16,128]{2,1,0:T(8,128)S(1)} %bitcast.169, f32[4,128,128]{2,1,0:T(8,128)} %fusion.117, pred[128,128]{1,0:T(8,128)(4,1)} %iota_compare_fusion, f32[128,4,16,32]{0,3,2,1:T(8,128)S(1)} %bitcast.156, f32[128,4,16]{0,2,1:T(8,128)S(1)} %bitcast.180, ...), kind=kOutput, calls=%fused_computation.15 | convolution fusion | flops 412270592 | bytes 2768896 | tf_op jit(solution)/shard_map/transpose(jvp(gjtr,rgjp->tgjp))/dot_general | solution.py:108
  205.2 1.4 convolution_add_fusion
  206.6 1.8 copy.73
  210.4 1.3 collective-permute-start.5
  211.7 6.2 %fusion.22 = f32[128,4,16,32]{0,3,2,1:T(8,128)} fusion(f32[4,16,128]{2,1,0:T(8,128)S(1)} %bitcast.170, f32[4,128,128]{2,1,0:T(8,128)} %fusion.117, pred[128,128]{1,0:T(8,128)(4,1)} %iota_compare_fusion, f32[128,4,16,32]{0,3,2,1:T(8,128)S(1)} %get-tuple-element.336), kind=kOutput, calls=%fused_computation.34 | convolution fusion | flops 405798912 | bytes 2408448 | tf_op jit(solution)/shard_map/transpose(jvp(gjtr,rgjp->tgjp))/dot_general | solution.py:108
  219.1 2.0 copy.77
  221.9 1.3 scatter-add.14
  223.2 89.9 %all-gather.6.cloned.1.call-done = f32[8,64,32,128]{3,2,1,0:T(8,128)} async-done(((f32[1,64,32,128]{3,2,1,0:T(8,128)}), f32[8,64,32,128]{3,2,1,0:T(8,128)}) %all-gather.6.cloned.1.call-update) | async-done | bytes 8388624 | tf_op jit(solution)/shard_map/all_gather | solution.py:18
  313.1 7.6 %rev.7 = f32[8,64,32,128]{3,2,1,0:T(8,128)} reverse(f32[8,64,32,128]{3,2,1,0:T(8,128)} %all-gather.6.cloned.1.call-done), dimensions={0} | reverse | bytes 16777216 | tf_op jit(solution)/shard_map/rev | solution.py:20
  320.7 15.3 %while.34 = (s32[]{:T(128)}, f32[64,32,128]{2,1,0:T(8,128)S(1)}, s32[]{:T(128)}, f32[8,64]{1,0:T(8,128)}, f32[8,64,32,128]{3,2,1,0:T(8,128)}, /*index=5*/s32[]{:T(128)}, s32[]{:T(128)}) while((s32[]{:T(128)}, f32[64,32,128]{2,1,0:T(8,128)S(1)}, s32[]{:T(128)}, f32[8,64]{1,0:T(8,128)}, f32[8,64,32,128]{3,2,1,0:T(8,128)}, ...), condition=%wide.region_6.7_spmd.clone, body=%wide.region_5.6_spmd.clone.sunk | while | flops 1048580 | bytes 3146601 | solution.py:30
  321.4 1.5 fusion.131
  323.6 1.5 fusion.131
  325.8 1.5 fusion.131
  328.0 1.5 fusion.131
  330.2 1.5 fusion.131
  332.4 1.5 fusion.131
  334.6 1.5 fusion.131
  336.1 2.3 multiply_reduce_fusion.1
  339.8 2.5 convolution_bitcast_fusion.4
  342.4 4.2 %multiply_reduce_fusion.3 = (f32[128,4,16]{0,2,1:T(8,128)S(1)}, f32[128,4,16]{0,2,1:T(8,128)}, f32[128,4,16,32]{0,3,2,1:T(8,128)}) fusion(f32[128,2048]{0,1:T(8,128)S(1)} %copy.59, f32[128,4,16,32]{0,3,2,1:T(8,128)} %fusion.22, f32[128,4,16]{0,2,1:T(8,128)S(1)} %bitcast.175, f32[128,4,16]{0,2,1:T(8,128)} %bitcast.181, ...), kind=kOutput, calls=%fused_computation.67 | convolution fusion | flops 404996096 | bytes 5636352 | tf_op jit(solution)/shard_map/transpose(jvp(tgjp,tgn->gjpn))/dot_general | solution.py:76
  347.8 1.2 reduce_window_sum.23
  349.0 1.5 fusion.31
  352.6 1.3 collective-permute-start.4
  353.9 1.6 copy.67
  356.5 1.3 collective-permute-start.3
  358.8 4.1 %collective-permute-done.3 = f32[3,2048]{1,0:T(4,128)S(1)} collective-permute-done((f32[3,2048]{1,0:T(4,128)S(1)}, f32[3,2048]{1,0:T(4,128)S(1)}, u32[]{:S(2)}, u32[]{:S(2)}) %collective-permute-start.3) | collective-permute-done | bytes 24608 | tf_op jit(solution)/shard_map/ppermute | solution.py:13
  (136 shorter events, 31.6 us)
Async XLA Ops:
  7.2 147.8 %all-gather.4.cloned.1.call-start = ((), (), s32[]{:S(2)}) async-start(), calls=%async_computation | async-start | bytes 9437184 | tf_op jit(solution)/shard_map/all_gather | solution.py:18
  8.0 16.8 %collective-permute-start = (bf16[3,2048]{1,0:T(4,128)(2,1)S(1)}, bf16[3,2048]{1,0:T(4,128)(2,1)S(1)}, u32[]{:S(2)}, u32[]{:S(2)}) collective-permute-start(bf16[3,2048]{1,0:T(4,128)(2,1)S(1)} %slice.203), channel_id=1, source_target_pairs={{0,2},{2,4},{4,6},{6,8},{8,10},{10,12},{12,14},{1,3},{3,5},{5,7},{... | collective-permute-start | bytes 36872 | tf_op jit(solution)/shard_map/ppermute | solution.py:13
  13.5 10.3 %collective-permute-start.2 = (bf16[3,512]{1,0:T(4,128)(2,1)S(1)}, bf16[3,512]{1,0:T(4,128)(2,1)S(1)}, u32[]{:S(2)}, u32[]{:S(2)}) collective-permute-start(bf16[3,512]{1,0:T(4,128)(2,1)S(1)} %slice.219), channel_id=1, source_target_pairs={{0,2},{2,4},{4,6},{6,8},{8,10},{10,12},{12,14},{1,3},{3,5},{5,7},{... | collective-permute-start | bytes 9224 | tf_op jit(solution)/shard_map/ppermute | solution.py:13
  17.7 0.8 copy-start.30
  18.5 175.8 %copy-start.12 = (f32[64,128]{1,0:T(8,128)}, f32[64,128]{1,0:T(8,128)S(1)}, u32[]{:S(2)}) copy-start(f32[64,128]{1,0:T(8,128)S(1)} %get-tuple-element.345) | copy-start | bytes 98308
  19.0 7.8 %copy-start.24 = (f32[64]{0:T(128)}, f32[64]{0:T(128)S(1)}, u32[]{:S(2)}) copy-start(f32[64]{0:T(128)S(1)} %get-tuple-element.309) | copy-start | bytes 772
  20.8 6.0 %copy-start.15 = (f32[1,2048]{1,0:T(1,128)}, f32[1,2048]{1,0:T(1,128)S(1)}, u32[]{:S(2)}) copy-start(f32[1,2048]{1,0:T(1,128)S(1)} %get-tuple-element.351) | copy-start | bytes 24580
  20.8 6.0 %copy-start.17 = (f32[1,2048]{1,0:T(1,128)}, f32[1,2048]{1,0:T(1,128)S(1)}, u32[]{:S(2)}) copy-start(f32[1,2048]{1,0:T(1,128)S(1)} %get-tuple-element.352) | copy-start | bytes 24580
  21.7 5.2 %copy-start.19 = (f32[1,512]{1,0:T(1,128)}, f32[1,512]{1,0:T(1,128)S(1)}, u32[]{:S(2)}) copy-start(f32[1,512]{1,0:T(1,128)S(1)} %get-tuple-element.357) | copy-start | bytes 6148
  21.7 5.2 %copy-start.20 = (f32[1,512]{1,0:T(1,128)}, f32[1,512]{1,0:T(1,128)S(1)}, u32[]{:S(2)}) copy-start(f32[1,512]{1,0:T(1,128)S(1)} %get-tuple-element.358) | copy-start | bytes 6148
  21.7 5.2 %copy-start.21 = (f32[1,512]{1,0:T(1,128)}, f32[1,512]{1,0:T(1,128)S(1)}, u32[]{:S(2)}) copy-start(f32[1,512]{1,0:T(1,128)S(1)} %get-tuple-element.359) | copy-start | bytes 6148
  21.7 5.2 %copy-start.22 = (f32[1,512]{1,0:T(1,128)}, f32[1,512]{1,0:T(1,128)S(1)}, u32[]{:S(2)}) copy-start(f32[1,512]{1,0:T(1,128)S(1)} %get-tuple-element.360) | copy-start | bytes 6148
  24.8 4.2 %copy-start.11 = (bf16[128,512]{1,0:T(8,128)(2,1)S(1)}, bf16[128,512]{1,0:T(8,128)(2,1)}, u32[]{:S(2)}) copy-start(bf16[128,512]{1,0:T(8,128)(2,1)} %param.26) | copy-start | bytes 393220
  24.8 8.8 %copy-start.29 = (f32[4,512]{1,0:T(4,128)S(1)}, f32[4,512]{1,0:T(4,128)}, u32[]{:S(2)}) copy-start(f32[4,512]{1,0:T(4,128)} %param.32) | copy-start | bytes 24580
  24.9 9.4 %copy-start.8 = (bf16[128,2048]{1,0:T(8,128)(2,1)S(1)}, bf16[128,2048]{1,0:T(8,128)(2,1)}, u32[]{:S(2)}) copy-start(bf16[128,2048]{1,0:T(8,128)(2,1)} %param.35) | copy-start | bytes 1572868
  24.9 9.4 %copy-start.28 = (f32[2048]{0:T(1024)S(1)}, f32[2048]{0:T(1024)}, u32[]{:S(2)}) copy-start(f32[2048]{0:T(1024)} %param.33) | copy-start | bytes 24580
  26.5 10.2 %copy-start.32 = (u32[32]{0:T(128)S(1)}, u32[32]{0:T(128)}, u32[]{:S(2)}) copy-start(u32[32]{0:T(128)} %constant.170) | copy-start | bytes 388
  29.0 284.2 %all-gather.6.cloned.1.call-start = ((), (), s32[]{:S(2)}) async-start(), calls=%async_computation.1 | async-start | bytes 9437184 | tf_op jit(solution)/shard_map/all_gather | solution.py:18
  29.6 34.1 %collective-permute-start.1 = (bf16[3,512]{1,0:T(4,128)(2,1)}, bf16[3,512]{1,0:T(4,128)(2,1)}, u32[]{:S(2)}, u32[]{:S(2)}) collective-permute-start(bf16[3,512]{1,0:T(4,128)(2,1)} %slice.211), channel_id=1, source_target_pairs={{0,2},{2,4},{4,6},{6,8},{8,10},{10,12},{12,14},{1,3},{3,5},{5,7},{... | collective-permute-start | bytes 9224 | tf_op jit(solution)/shard_map/ppermute | solution.py:13
  174.1 4.6 %copy-start.2 = (f32[128,2048]{0,1:T(8,128)S(1)}, f32[128,2048]{0,1:T(8,128)}, u32[]{:S(2)}) copy-start(f32[128,2048]{0,1:T(8,128)} %copy.64) | copy-start | bytes 3145732
  174.2 4.6 %copy-start.10 = (f32[4,128,128]{2,1,0:T(8,128)S(1)}, f32[4,128,128]{2,1,0:T(8,128)}, u32[]{:S(2)}) copy-start(f32[4,128,128]{2,1,0:T(8,128)} %fusion.117) | copy-start | bytes 786436
  174.2 4.6 %copy-start.23 = (pred[128,128]{1,0:T(8,128)(4,1)S(1)}, pred[128,128]{1,0:T(8,128)(4,1)}, u32[]{:S(2)}) copy-start(pred[128,128]{1,0:T(8,128)(4,1)} %iota_compare_fusion) | copy-start | bytes 49156
  174.2 4.5 %copy-start.27 = (f32[4,16]{1,0:T(4,128)S(1)}, f32[4,16]{1,0:T(4,128)}, u32[]{:S(2)}) copy-start(f32[4,16]{1,0:T(4,128)} %mul.539) | copy-start | bytes 772
  175.7 1.0 copy-start
  185.6 2.2 copy-start.3
  194.3 10.9 %copy-start.4 = (f32[128,4,128]{0,2,1:T(8,128)S(1)}, f32[128,4,128]{0,2,1:T(8,128)}, u32[]{:S(2)}) copy-start(f32[128,4,128]{0,2,1:T(8,128)} %copy.72) | copy-start | bytes 786436
  205.2 1.4 copy-start.5
  210.3 7.5 %copy-start.7 = (f32[131,512]{1,0:T(8,128)}, f32[131,512]{1,0:T(8,128)S(1)}, u32[]{:S(2)}) copy-start(f32[131,512]{1,0:T(8,128)S(1)} %multiply_add_fusion.3) | copy-start | bytes 804868
  210.4 10.8 %collective-permute-start.5 = (f32[3,512]{1,0:T(4,128)S(1)}, f32[3,512]{1,0:T(4,128)S(1)}, u32[]{:S(2)}, u32[]{:S(2)}) collective-permute-start(f32[3,512]{1,0:T(4,128)S(1)} %slice.269), channel_id=1, source_target_pairs={{2,0},{4,2},{6,4},{8,6},{10,8},{12,10},{14,12},{3,1},{5,3},{7,5},{... | collective-permute-start | bytes 18440 | tf_op jit(solution)/shard_map/ppermute | solution.py:13
  338.4 8.1 %copy-start.6 = (f32[64,128]{1,0:T(8,128)S(1)}, f32[64,128]{1,0:T(8,128)}, u32[]{:S(2)}) copy-start(f32[64,128]{1,0:T(8,128)} %param.27) | copy-start | bytes 98308
  339.1 7.4 %copy-start.25 = (f32[64]{0:T(128)S(1)}, f32[64]{0:T(128)}, u32[]{:S(2)}) copy-start(f32[64]{0:T(128)} %copy-done.24) | copy-start | bytes 772
  346.5 8.9 %copy-start.1 = (f32[128,2048]{1,0:T(8,128)S(1)}, f32[128,2048]{1,0:T(8,128)}, u32[]{:S(2)}) copy-start(f32[128,2048]{1,0:T(8,128)} %get-tuple-element.338) | copy-start | bytes 3145732
  347.8 8.2 %copy-start.16 = (f32[1,2048]{1,0:T(1,128)S(1)}, f32[1,2048]{1,0:T(1,128)}, u32[]{:S(2)}) copy-start(f32[1,2048]{1,0:T(1,128)} %copy-done.15) | copy-start | bytes 24580
  347.8 8.2 %copy-start.18 = (f32[1,2048]{1,0:T(1,128)S(1)}, f32[1,2048]{1,0:T(1,128)}, u32[]{:S(2)}) copy-start(f32[1,2048]{1,0:T(1,128)} %copy-done.17) | copy-start | bytes 24580
  351.7 6.0 %copy-start.13 = (f32[128,4,16]{0,2,1:T(8,128)S(1)}, f32[128,4,16]{0,2,1:T(8,128)}, u32[]{:S(2)}) copy-start(f32[128,4,16]{0,2,1:T(8,128)} %get-tuple-element.308) | copy-start | bytes 98308
  351.7 6.0 %copy-start.26 = (f32[64]{0:T(128)S(1)}, f32[64]{0:T(128)}, u32[]{:S(2)}) copy-start(f32[64]{0:T(128)} %copy-done.24) | copy-start | bytes 772
  351.7 6.0 %copy-start.31 = (f32[64]{0:T(128)S(1)}, f32[64]{0:T(128)}, u32[]{:S(2)}) copy-start(f32[64]{0:T(128)} %copy-done.30) | copy-start | bytes 772
  352.6 6.0 %collective-permute-start.4 = (f32[3,512]{1,0:T(4,128)S(1)}, f32[3,512]{1,0:T(4,128)S(1)}, u32[]{:S(2)}, u32[]{:S(2)}) collective-permute-start(f32[3,512]{1,0:T(4,128)S(1)} %slice.266), channel_id=1, source_target_pairs={{2,0},{4,2},{6,4},{8,6},{10,8},{12,10},{14,12},{3,1},{5,3},{7,5},{... | collective-permute-start | bytes 18440 | tf_op jit(solution)/shard_map/ppermute | solution.py:13
  356.5 6.4 %collective-permute-start.3 = (f32[3,2048]{1,0:T(4,128)S(1)}, f32[3,2048]{1,0:T(4,128)S(1)}, u32[]{:S(2)}, u32[]{:S(2)}) collective-permute-start(f32[3,2048]{1,0:T(4,128)S(1)} %slice.263), channel_id=1, source_target_pairs={{2,0},{4,2},{6,4},{8,6},{10,8},{12,10},{14,12},{3,1},{5,3},{7,5},{... | collective-permute-start | bytes 73736 | tf_op jit(solution)/shard_map/ppermute | solution.py:13
  358.8 4.3 %copy-start.14 = (bf16[128,512]{1,0:T(8,128)(2,1)}, bf16[128,512]{1,0:T(8,128)(2,1)S(1)}, u32[]{:S(2)}) copy-start(bf16[128,512]{1,0:T(8,128)(2,1)S(1)} %scatter-add.11) | copy-start | bytes 393220
  363.1 0.8 copy-start.9
Sparse Core Ops, SparseCore 0:
  29.1 125.8 all-gather.3
  190.1 123.0 all-gather.5
where the time goes:
time: 373 us; the launch traced here: 371 us
  waiting for transfers between devices  176 us (47%)
  other arithmetic  57.9 us (16%)
  matrix products  45 us (12%)
  local copies, waits for them, and re-layouts  40.7 us (11%)
  blocking collectives  18.8 us (5%)
  starting transfers between devices  16.2 us (4%)
  between operations  15.4 us (4%)
    all_gather x2, waiting for transfers between devices, prefix_2(): pieces = jax.tree.map(lambda part: lax.all_gather(part, axis), value)  172 us
    select_n x21, other arithmetic, hop(): jnp.where(position < mine, new, old)  29.2 us
    dot_general x3, matrix products, block_output(): within = jnp.einsum('gjtr,rgjp->tgjp', mixing, scaled, precision=EXACT)  23.9 us
    unnamed x1, blocking collectives  18.8 us
    ppermute x6, starting transfers between devices, from_behind(): return lax.ppermute(array, axis, pairs)  16.1 us
    rev x2, local copies, waits for them, and re-layouts, prefix_2(): pieces = jax.tree.map(lambda part: part[::-1], pieces)  8.87 us
    dot_general x3, matrix products, block_summary(): summary = jnp.einsum('tgjp,tgn->gjpn', scaled, b_groups, precision=EXACT)  8.75 us
  transfers between devices with their start and end apart: 8, of which 3 were waited for; matrix products, arithmetic and copies ran while one was open for 17% of the time, Pallas kernels for 0%

commit v1 on v0

v1 whole, which is shorter than its diff:
```python
import functools

import jax
import jax.numpy as jnp
from jax import lax
from jax.experimental import pallas as pl
from jax.experimental.pallas import tpu as pltpu
from jax.sharding import PartitionSpec as P

EPS = 1e-05
EXACT = lax.Precision.HIGHEST
MESH = pl.DeviceIdType.MESH
F32, BF16 = jnp.float32, jnp.bfloat16
NN, NT, TN = (((1,), (0,)), ((1,), (1,)), ((0,), (0,)))
BLOCK = 4


def split(a):
    high = a.astype(BF16)
    return high, (a - high.astype(F32)).astype(BF16)


def dot(a, b, dims):
    return lax.dot_general(a, b, (dims, ((), ())), preferred_element_type=F32)


def dot3(a, b, dims):
    (ah, al), (bh, bl) = a, b
    return dot(ah, bh, dims) + (dot(ah, bl, dims) + dot(al, bh, dims))


def exact(a, b, dims=NN):
    return lax.dot_general(a, b, (dims, ((), ())), precision=EXACT, preferred_element_type=F32)


def iota(shape, dim):
    return lax.broadcasted_iota(jnp.int32, shape, dim)


def sigmoid(v):
    return 1.0 / (1.0 + jnp.exp(-v))


def kernel(
    x_ref, z_ref, b_ref, c_ref, dt_ref, alog_ref, skip_ref, wx_ref, wb_ref, wc_ref, gain_ref, state_ref, go_ref,
    gx_ref, gz_ref, gb_ref, gc_ref, gdt_ref,
    halo_x, halo_b, halo_c, ext, pre_x, pre_b, pre_c, sig, bco, cco, step_row, cum_row, acol, skcol, cum_t,
    step_x, ecum_x, e_x, dec_x, summ, ent, exi, d_ent, d_exi, back, dm_s, r1_s, dsc_s, dbs, dcs, mask_s,
    gp, ghalo, gsend, gpb,
    hs_sem, hr_sem, fs_sem, fr_sem, bs_sem, br_sem, gs_sem, gr_sem,
):
    me, peers = lax.axis_index("seq"), lax.axis_size("seq")
    first, last = me == 0, me == peers - 1
    tok, chan = x_ref.shape
    heads = dt_ref.shape[0]
    hd = chan // heads
    nn = state_ref.shape[1]
    groups = b_ref.shape[1] // nn
    per = heads // groups
    gw = chan // groups
    bw = BLOCK * hd
    blocks = gw // bw
    taps = wx_ref.shape[0]
    chunks = groups * blocks
    before, after = {"seq": jnp.maximum(me - 1, 0)}, {"seq": jnp.minimum(me + 1, peers - 1)}

    barrier = pltpu.get_barrier_semaphore()

    @pl.when(jnp.logical_not(first))
    def _():
        pl.semaphore_signal(barrier, inc=1, device_id=before, device_id_type=MESH)

    @pl.when(jnp.logical_not(last))
    def _():
        pl.semaphore_signal(barrier, inc=1, device_id=after, device_id_type=MESH)

    pl.semaphore_wait(barrier, jnp.minimum(me, 1) + jnp.minimum(peers - 1 - me, 1))

    def remote(src, dst, ssem, rsem, to):
        return pltpu.make_async_remote_copy(
            src_ref=src, dst_ref=dst, send_sem=ssem, recv_sem=rsem, device_id=to, device_id_type=MESH
        )

    halos = [
        remote(src.at[pl.ds(tok - 16, 16), :], dst, hs_sem.at[i], hr_sem.at[i], after)
        for i, (src, dst) in enumerate(((x_ref, halo_x), (b_ref, halo_b), (c_ref, halo_c)))
    ]

    @pl.when(jnp.logical_not(last))
    def _():
        for copy in halos:
            copy.start()

    eye_h = iota((heads, heads), 0) == iota((heads, heads), 1)

    def column(row):
        return jnp.broadcast_to(
            jnp.sum(jnp.where(eye_h, row, 0.0), axis=1, keepdims=True), (heads, 128)
        )

    acol[...] = column(jnp.exp(alog_ref[...]))
    skcol[...] = column(skip_ref[...])
    steps_all = jnp.log1p(jnp.exp(dt_ref[...]))
    step_row[...] = steps_all
    upto = (iota((tok, tok), 0) <= iota((tok, tok), 1)).astype(F32)
    cum_row[...] = exact(-acol[...] * steps_all, upto)

    @pl.when(first)
    def _():
        halo_x[...] = jnp.zeros_like(halo_x)
        halo_b[...] = jnp.zeros_like(halo_b)
        halo_c[...] = jnp.zeros_like(halo_c)

    @pl.when(jnp.logical_not(first))
    def _():
        for copy in halos:
            copy.wait_recv()

    spread = (iota((per, gw), 1) // hd == iota((per, gw), 0)).astype(F32)
    spread_b = spread.astype(BF16)
    lane_of = iota((tok, bw), 1) // hd
    lower = iota((tok, tok), 0) >= iota((tok, tok), 1)
    upper = iota((tok, tok), 0) <= iota((tok, tok), 1)

    def conv(src, halo, w_ref, at, width):
        cols = pl.ds(at, width)
        ext[0:8, :width] = halo[:, cols].astype(F32)[8:16]
        ext[8 : 8 + tok, :width] = src[:, cols].astype(F32)
        w = w_ref[:, cols]
        total = w[0:1] * ext[9 - taps : 9 - taps + tok, :width]
        for k in range(1, taps):
            total = total + w[k : k + 1] * ext[9 - taps + k : 9 - taps + k + tok, :width]
        return total

    def local(g, _):
        at, nat, hat = (pl.multiple_of(g * w, w) for w in (gw, nn, per))
        cols, ncols, rows = pl.ds(at, gw), pl.ds(nat, nn), pl.ds(hat, per)
        px = conv(x_ref, halo_x, wx_ref, at, gw)
        pre_x[:, cols] = px
        s = px * sigmoid(px)
        sig[:, cols] = s
        pb = conv(b_ref, halo_b, wb_ref, nat, nn)
        pre_b[:, ncols] = pb
        bv = pb * sigmoid(pb)
        bco[:, ncols] = bv
        pc = conv(c_ref, halo_c, wc_ref, nat, nn)
        pre_c[:, ncols] = pc
        cco[:, ncols] = pc * sigmoid(pc)
        cum, st = cum_row[rows, :], step_row[rows, :]
        cl = cum[:, tok - 1 : tok]
        cum_t[g] = jnp.concatenate([cum, jnp.zeros((128 - per, tok), F32)], axis=0).T
        sx = exact(st, spread, TN)
        step_x[:, cols] = sx
        ecum_x[:, cols] = exact(jnp.exp(cum), spread, TN)
        ex = exact(jnp.exp(cl - cum), spread, TN)
        e_x[:, cols] = ex
        hrows = pl.ds(at, gw)
        dec_x[hrows, :] = exact(spread, jnp.broadcast_to(jnp.exp(cl), (per, nn)), TN)
        summ[hrows, :] = dot3(split(s * sx * ex), split(bv), TN)
        return 0

    lax.fori_loop(0, groups, local, 0)

    @pl.when(first)
    def _():
        ent[...] = state_ref[...]

    def piece(k):
        return pl.ds(pl.multiple_of(k * bw, bw), bw)

    def forward_copy(k):
        return remote(exi.at[piece(k), :], ent.at[piece(k), :], fs_sem.at[k], fr_sem.at[k], after)

    def forward(k, _):
        @pl.when(jnp.logical_not(first))
        def _():
            forward_copy(k).wait_recv()

        rows = piece(k)
        exi[rows, :] = dec_x[rows, :] * ent[rows, :] + summ[rows, :]

        @pl.when(jnp.logical_not(last))
        def _():
            forward_copy(k).start()

        return 0

    lax.fori_loop(0, chunks, forward, 0)

    def backward_copy(k):
        return remote(back.at[piece(k), :], d_exi.at[piece(k), :], bs_sem.at[k], br_sem.at[k], before)

    def backward(k, _):
        @pl.when(jnp.logical_not(last))
        def _():
            backward_copy(k).wait_recv()

        @pl.when(jnp.logical_not(first))
        def _():
            rows = piece(k)
            back[rows, :] = dec_x[rows, :] * d_exi[rows, :] + d_ent[rows, :]
            backward_copy(k).start()

        return 0

    @pl.when(last)
    def _():
        d_exi[...] = jnp.zeros_like(d_exi)

    def output(g, _):
        at, nat, hat = (pl.multiple_of(g * w, w) for w in (gw, nn, per))
        cols, ncols, rows = pl.ds(at, gw), pl.ds(nat, nn), pl.ds(hat, per)
        bs, cs = split(bco[:, ncols]), split(cco[:, ncols])
        scores = dot3(cs, bs, NT)
        scores_t = dot3(bs, cs, NT)
        ents = split(ent[pl.ds(at, gw), :])
        s = sig[:, cols]
        sc = step_x[:, cols] * s
        cum, cum_c = cum_row[rows, :], cum_t[g]
        within = []
        for j in range(blocks):
            sc4 = sc[:, j * bw : (j + 1) * bw]
            ms, rs = [], []
            for i in range(BLOCK):
                h = j * BLOCK + i
                gap = cum_c[:, h : h + 1] - cum[h : h + 1, :]
                mask = jnp.exp(jnp.where(lower, gap, -1e30))
                mask_s[h] = mask
                ms.append(split(scores * mask))
                rs.append(split(jnp.where(lane_of == i, sc4, 0.0)))
            m = tuple(jnp.concatenate([v[q] for v in ms], axis=1) for q in (0, 1))
            r = tuple(jnp.concatenate([v[q] for v in rs], axis=0) for q in (0, 1))
            within.append(dot3(m, r, NN))
        inner = jnp.concatenate(within, axis=1) + ecum_x[:, cols] * dot3(cs, ents, NT)
        skx = jnp.sum(spread * skcol[rows, 0:1], axis=0, keepdims=True)
        mixed = inner + skx * s
        z = z_ref[:, cols].astype(F32)
        zs = sigmoid(z)
        sz = z * zs
        gated = mixed * sz
        inv = lax.rsqrt(jnp.mean(gated * gated, axis=1, keepdims=True) + EPS)
        dn = go_ref[:, cols].astype(F32) * gain_ref[:, cols]
        unit = gated * inv
        dg = inv * (dn - unit * jnp.mean(dn * unit, axis=1, keepdims=True))
        gz_ref[:, cols] = (dg * mixed * (zs + sz * (1.0 - zs))).astype(BF16)
        dm = dg * sz
        dm_s[:, cols] = dm
        r1_s[rows, :] = sum(dot(spread_b, v, NT) for v in split(dm * inner))
        dcar = split(dm * ecum_x[:, cols])
        d_ent[pl.ds(at, gw), :] = dot3(dcar, cs, TN)

        @pl.when(last)
        def _():
            lax.fori_loop(g * blocks, (g + 1) * blocks, backward, 0)

        ds = jnp.zeros((tok, tok), F32)
        for j in range(blocks):
            dm4 = dm[:, j * bw : (j + 1) * bw]
            scs = split(sc[:, j * bw : (j + 1) * bw])
            ms, rs = [], []
            for i in range(BLOCK):
                h = j * BLOCK + i
                gap = cum[h : h + 1, :] - cum_c[:, h : h + 1]
                ms.append(split(scores_t * jnp.exp(jnp.where(upper, gap, -1e30))))
                rs.append(split(jnp.where(lane_of == i, dm4, 0.0)))
                ds = ds + dot3(rs[-1], scs, NT) * mask_s[h]
            m = tuple(jnp.concatenate([v[q] for v in ms], axis=1) for q in (0, 1))
            r = tuple(jnp.concatenate([v[q] for v in rs], axis=0) for q in (0, 1))
            dsc_s[:, pl.ds(at + j * bw, bw)] = dot3(m, r, NN)
        dss = split(ds)
        dcs[:, ncols] = dot3(dss, bs, NN) + dot3(dcar, ents, NN)
        dbs[:, ncols] = dot3(dss, cs, TN)
        return 0

    lax.fori_loop(0, groups, output, 0)

    from_t = (iota((tok, tok), 0) >= iota((tok, tok), 1)).astype(F32)

    def grad_copy(g):
        return remote(gsend.at[g], ghalo.at[g], gs_sem.at[g], gr_sem.at[g], before)

    def silu_back(grad, pre):
        s = sigmoid(pre)
        return grad * (s + pre * s * (1.0 - s))

    def closing(g, _):
        at, nat, hat = (pl.multiple_of(g * w, w) for w in (gw, nn, per))
        cols, ncols, rows = pl.ds(at, gw), pl.ds(nat, nn), pl.ds(hat, per)

        @pl.when(jnp.logical_not(last))
        def _():
            lax.fori_loop(g * blocks, (g + 1) * blocks, backward, 0)

        grad = d_exi[pl.ds(at, gw), :]
        grads = split(grad)
        s, sx, ex = sig[:, cols], step_x[:, cols], e_x[:, cols]
        bs = split(bco[:, ncols])
        both = dsc_s[:, cols] + ex * dot3(bs, grads, NT)
        skx = jnp.sum(spread * skcol[rows, 0:1], axis=0, keepdims=True)
        gpx = silu_back(sx * both + skx * dm_s[:, cols], pre_x[:, cols])
        db = dbs[:, ncols] + dot3(split(s * sx * ex), grads, NN)
        gpbv = silu_back(db, pre_b[:, ncols])
        gpcv = silu_back(dcs[:, ncols], pre_c[:, ncols])
        gp[0:tok, cols] = gpx
        gpb[g, 0:tok, 0:nn] = gpbv
        gpb[g, 0:tok, nn : 2 * nn] = gpcv

        @pl.when(jnp.logical_not(first))
        def _():
            gsend[g, :, 0:gw] = gpx[0:8]
            gsend[g, :, gw : gw + nn] = gpbv[0:8]
            gsend[g, :, gw + nn :] = gpcv[0:8]
            grad_copy(g).start()

        u = sum(dot(spread_b, v, NT) for v in split(s * both))
        lane = jnp.sum(exact(spread, grad * exi[pl.ds(at, gw), :]), axis=1, keepdims=True)
        st = step_row[rows, :]
        d_rate = exact(r1_s[rows, :] - st * u, from_t) + lane
        gdt_ref[rows, :] = (u - acol[rows, :] * d_rate) * sigmoid(dt_ref[rows, :])
        return 0

    lax.fori_loop(0, groups, closing, 0)

    @pl.when(last)
    def _():
        ghalo[...] = jnp.zeros_like(ghalo)

    def finish(g, _):
        at, nat = (pl.multiple_of(g * w, w) for w in (gw, nn))
        cols, ncols = pl.ds(at, gw), pl.ds(nat, nn)

        @pl.when(jnp.logical_not(last))
        def _():
            grad_copy(g).wait_recv()

        gp[tok : tok + 8, cols] = ghalo[g, :, 0:gw]
        gpb[g, tok : tok + 8, :] = ghalo[g, :, gw:]
        tx = tb = tc = 0.0
        for k in range(taps):
            row = slice(taps - 1 - k, taps - 1 - k + tok)
            tx = tx + wx_ref[k : k + 1, cols] * gp[row, cols]
            tb = tb + wb_ref[k : k + 1, ncols] * gpb[g, row, 0:nn]
            tc = tc + wc_ref[k : k + 1, ncols] * gpb[g, row, nn : 2 * nn]
        gx_ref[:, cols] = tx.astype(BF16)
        gb_ref[:, ncols] = tb.astype(BF16)
        gc_ref[:, ncols] = tc.astype(BF16)
        return 0

    lax.fori_loop(0, groups, finish, 0)

    @pl.when(jnp.logical_not(last))
    def _():
        for copy in halos:
            copy.wait_send()

        def drain(k, _):
            forward_copy(k).wait_send()
            return 0

        lax.fori_loop(0, chunks, drain, 0)

    @pl.when(jnp.logical_not(first))
    def _():
        def drain(k, _):
            backward_copy(k).wait_send()
            return 0

        lax.fori_loop(0, chunks, drain, 0)

        def drain_halo(g, _):
            grad_copy(g).wait_send()
            return 0

        lax.fori_loop(0, groups, drain_halo, 0)


def per_device(
    x_stream, z_stream, b_stream, c_stream, dt_raw, a_log, skip_coef, conv_x, conv_b, conv_c, norm_gain, state_in, grad_out
):
    tok, chan = x_stream.shape
    heads, hd, nn = state_in.shape
    wide = b_stream.shape[1]
    groups = wide // nn
    per, gw = heads // groups, chan // groups
    chunks = chan // (BLOCK * hd)
    dma = pltpu.SemaphoreType.DMA

    def v(*shape, dtype=F32):
        return pltpu.VMEM(shape, dtype)

    scratch = [
        v(16, chan, dtype=BF16), v(16, wide, dtype=BF16), v(16, wide, dtype=BF16),
        v(tok + 8, gw), v(tok, chan), v(tok, wide), v(tok, wide), v(tok, chan), v(tok, wide), v(tok, wide),
        v(heads, tok), v(heads, tok), v(heads, 128), v(heads, 128), v(groups, tok, 128),
        v(tok, chan), v(tok, chan), v(tok, chan), v(chan, nn),
        v(chan, nn), v(chan, nn), v(chan, nn), v(chan, nn), v(chan, nn), v(chan, nn),
        v(tok, chan), v(heads, tok), v(tok, chan), v(tok, wide), v(tok, wide), v(per, tok, tok),
        v(tok + 8, chan), v(groups, 8, gw + 2 * nn), v(groups, 8, gw + 2 * nn), v(groups, tok + 8, 2 * nn),
        dma((3,)), dma((3,)), dma((chunks,)), dma((chunks,)), dma((chunks,)), dma((chunks,)),
        dma((groups,)), dma((groups,)),
    ]
    vmem = pl.BlockSpec(memory_space=pltpu.VMEM)
    outs = [
        jax.ShapeDtypeStruct(a.shape, a.dtype) for a in (x_stream, z_stream, b_stream, c_stream, dt_raw)
    ]
    return pl.pallas_call(
        kernel,
        out_shape=outs,
        in_specs=[vmem] * 13,
        out_specs=[vmem] * 5,
        scratch_shapes=scratch,
        compiler_params=pltpu.CompilerParams(
            collective_id=0, has_side_effects=True, vmem_limit_bytes=56 * 2**20
        ),
    )(
        x_stream, z_stream, b_stream, c_stream, dt_raw, a_log.reshape(1, heads), skip_coef.reshape(1, heads),
        conv_x, conv_b, conv_c, norm_gain.reshape(1, chan), state_in.reshape(heads * hd, nn), grad_out,
    )


def solution(mesh):
    rows = P(("group", "seq"), "head")
    turned = P("head", ("group", "seq"))
    taps = P(None, "head")
    return jax.shard_map(
        per_device,
        mesh=mesh,
        in_specs=(
            rows, rows, rows, rows, turned, P(("group", "head")), P("head"), taps, taps, taps, P("head"),
            P(("group", "head"), None, None), rows,
        ),
        out_specs=(rows, rows, rows, rows, turned),
        check_vma=False,
    )
```

time: 373 us -> 119 us (0.32)
  waiting for transfers between devices: 176 us -> 0 us
  Pallas kernels: 0 us -> 113 us
  other arithmetic: 57.9 us -> 0 us
  matrix products: 45 us -> 0 us
  local copies, waits for them, and re-layouts: 40.7 us -> 5.29 us
  blocking collectives: 18.8 us -> 0 us
  starting transfers between devices: 16.2 us -> 0 us
  between operations: 15.4 us -> 0.66 us
    all_gather x2 -> x0, waiting for transfers between devices: 172 us -> none  [prefix_2(): pieces = jax.tree.map(lambda part: lax.all_gather(part, axis), value)]
    pallas_call x0 -> x1, Pallas kernels: none -> 113 us  [per_device(): pl.pallas_call(kernel, out_shape=outs, in_specs=[vmem] * 13, out_specs=[v...]
    dot_general x12 -> x0, matrix products: 45 us -> none  [the longest x3 23.9 us: block_output(): within = jnp.einsum('gjtr,rgjp->tgjp', mixing, scaled, precision=EXACT)]
    select_n x22 -> x0, other arithmetic: 30 us -> none  [the longest x21 29.2 us: hop(): jnp.where(position < mine, new, old)]
    unnamed x1 -> x0, blocking collectives: 18.8 us -> none
    ppermute x6 -> x0, starting transfers between devices: 16.1 us -> none  [from_behind(): return lax.ppermute(array, axis, pairs)]
    rev x2 -> x0, local copies, waits for them, and re-layouts: 8.87 us -> none  [prefix_2(): pieces = jax.tree.map(lambda part: part[::-1], pieces)]
    reshape x7 -> x0, local copies, waits for them, and re-layouts: 8.67 us -> none  [the longest x3 5.32 us: block_output(): c_groups = c_coef.reshape(length, group_count, state_width)]
  transfers between devices with their start and end apart: 8 -> 0, of which waited for: 3 -> 0; matrix products, arithmetic and copies ran while one was open for 17% -> 0% of each run, Pallas kernels for 0% -> 0%
where the time goes in v1:
time: 119 us; the launch traced here: 118 us
  Pallas kernels  113 us (95%)
  local copies, waits for them, and re-layouts  5.29 us (4%)
    pallas_call x1, Pallas kernels, per_device(): pl.pallas_call(kernel, out_shape=outs, in_specs=[vmem] * 13, out_specs=[v...  113 us
    unnamed x13, local copies, waits for them, and re-layouts  5.29 us

profile of v1, /device:TPU:0, one launch (start us, length us, event | category | flops | bytes accessed | tf_op | source)
XLA Modules:
  0.0 118.5 jit_solution(2987533599840311450)
XLA Ops:
  0.6 112.5 %shard_map.164 = (bf16[128,2048]{1,0:T(8,128)(2,1)}, bf16[128,2048]{1,0:T(8,128)(2,1)}, bf16[128,512]{1,0:T(8,128)(2,1)}, bf16[128,512]{1,0:T(8,128)(2,1)}, f32[64,128]{1,0:T(8,128)}) custom-call(bf16[128,2048]{1,0:T(8,128)(2,1)} %x_ref.1, bf16[128,2048]{1,0:T(8,128)(2,1)} %z_ref.1, bf16[128,512]{1,0:T(8,128)(2,1)} %b_ref.1, bf16[128,512]{1,0:T(8,128)(2,1)} %c_ref.1, ...), custom_call_target="tpu_custom_call" | custom-call | tf_op jit(solution)/shard_map/pallas_call | solution.py:406
  113.2 0.0 copy-start
  113.2 1.9 %copy.23 = bf16[128,2048]{1,0:T(8,128)(2,1)} copy(bf16[128,2048]{1,0:T(8,128)(2,1)} %get-tuple-element.10) | data formatting | bytes 1048576
  115.1 0.0 copy-done
  115.1 0.0 copy-start.2
  115.1 0.8 copy.24
  115.9 0.2 copy-done.2
  116.1 0.0 copy-start.1
  116.1 0.7 copy.25
  116.8 0.3 copy-done.1
  117.1 0.0 copy-start.3
  117.1 0.7 copy.26
  117.7 0.1 copy-done.3
  117.8 0.6 copy.27
Async XLA Ops:
  113.2 2.0 %copy-start = (bf16[128,2048]{1,0:T(8,128)(2,1)S(1)}, bf16[128,2048]{1,0:T(8,128)(2,1)}, u32[]{:S(2)}) copy-start(bf16[128,2048]{1,0:T(8,128)(2,1)} %get-tuple-element.11) | copy-start | bytes 1572868
  115.1 1.0 copy-start.2
  116.1 1.0 copy-start.1
  117.1 0.8 copy-start.3

commit v2 on v1

--- a/solution.py
+++ b/solution.py
@@ -45,9 +45,10 @@
     x_ref, z_ref, b_ref, c_ref, dt_ref, alog_ref, skip_ref, wx_ref, wb_ref, wc_ref, gain_ref, state_ref, go_ref,
     gx_ref, gz_ref, gb_ref, gc_ref, gdt_ref,
     halo_x, halo_b, halo_c, ext, pre_x, pre_b, pre_c, sig, bco, cco, step_row, cum_row, acol, skcol, cum_t,
-    step_x, ecum_x, e_x, dec_x, summ, ent, exi, d_ent, d_exi, back, dm_s, r1_s, dsc_s, dbs, dcs, mask_s,
+    step_x, ecum_x, e_x, dec_x, pdec_x, decs, pdecs,
+    summ, psum, ebuf, ent, f_out, f_other, d_ent, pd_ent, gbuf, d_exi, b_out, b_other, dm_s, r1_s, dsc_s, dbs, dcs, mask_s,
     gp, ghalo, gsend, gpb,
-    hs_sem, hr_sem, fs_sem, fr_sem, bs_sem, br_sem, gs_sem, gr_sem,
+    hs_sem, hr_sem, chunk_sem, gs_sem, gr_sem,
 ):
     me, peers = lax.axis_index("seq"), lax.axis_size("seq")
     first, last = me == 0, me == peers - 1
@@ -61,20 +62,28 @@
     bw = BLOCK * hd
     blocks = gw // bw
     taps = wx_ref.shape[0]
-    chunks = groups * blocks
+    half = blocks // 2
+    own = groups * half
+    side, pair, pairs = lax.rem(me, 2), me // 2, peers // 2
+    first_pair, last_pair = pair == 0, pair == pairs - 1
+    left = side == 0
+    partner = {"seq": me + 1 - 2 * side}
+    pair_before, pair_after = {"seq": jnp.maximum(me - 2, 0)}, {"seq": jnp.minimum(me + 2, peers - 1)}
     before, after = {"seq": jnp.maximum(me - 1, 0)}, {"seq": jnp.minimum(me + 1, peers - 1)}
 
     barrier = pltpu.get_barrier_semaphore()
 
-    @pl.when(jnp.logical_not(first))
-    def _():
-        pl.semaphore_signal(barrier, inc=1, device_id=before, device_id_type=MESH)
-
-    @pl.when(jnp.logical_not(last))
-    def _():
-        pl.semaphore_signal(barrier, inc=1, device_id=after, device_id_type=MESH)
-
-    pl.semaphore_wait(barrier, jnp.minimum(me, 1) + jnp.minimum(peers - 1 - me, 1))
+    for there, to in ((first, before), (last, after), (first_pair, pair_before), (last_pair, pair_after)):
+
+        @pl.when(jnp.logical_not(there))
+        def _(to=to):
+            pl.semaphore_signal(barrier, inc=1, device_id=to, device_id_type=MESH)
+
+    ahead = peers - 1 - me
+    pl.semaphore_wait(
+        barrier,
+        jnp.minimum(me, 1) + jnp.minimum(me // 2, 1) + jnp.minimum(ahead, 1) + jnp.minimum(ahead // 2, 1),
+    )
 
     def remote(src, dst, ssem, rsem, to):
         return pltpu.make_async_remote_copy(
@@ -103,7 +112,11 @@
     steps_all = jnp.log1p(jnp.exp(dt_ref[...]))
     step_row[...] = steps_all
     upto = (iota((tok, tok), 0) <= iota((tok, tok), 1)).astype(F32)
-    cum_row[...] = exact(-acol[...] * steps_all, upto)
+    cum_all = exact(-acol[...] * steps_all, upto)
+    cum_row[...] = cum_all
+    decs[...] = jnp.broadcast_to(jnp.exp(cum_all[:, tok - 1 : tok]), (heads, 128))
+    dec_copy = remote(decs, pdecs, hs_sem.at[3], hr_sem.at[3], partner)
+    dec_copy.start()
 
     @pl.when(first)
     def _():
@@ -131,6 +144,38 @@
         for k in range(1, taps):
             total = total + w[k : k + 1] * ext[9 - taps + k : 9 - taps + k + tok, :width]
         return total
+
+    def piece(k):
+        return pl.ds(pl.multiple_of(k * bw, bw), bw)
+
+    def moved(way, src, dst, k, to):
+        return remote(
+            src.at[piece(k), :], dst.at[piece(k), :], chunk_sem.at[way, 0, k], chunk_sem.at[way, 1, k], to
+        )
+
+    def mine(m):
+        return m // half * blocks + side * half + lax.rem(m, half)
+
+    def theirs(m):
+        return m // half * blocks + (1 - side) * half + lax.rem(m, half)
+
+    def summary_copy(k):
+        return moved(0, summ, psum, k, partner)
+
+    def forward_copy(k):
+        return moved(1, f_out, ebuf, k, pair_after)
+
+    def enter_copy(k):
+        return moved(2, f_other, ent, k, partner)
+
+    def grad_out_copy(k):
+        return moved(3, d_ent, pd_ent, k, partner)
+
+    def backward_copy(k):
+        return moved(4, b_out, gbuf, k, pair_before)
+
+    def exit_copy(k):
+        return moved(5, b_other, d_exi, k, partner)
 
     def local(g, _):
         at, nat, hat = (pl.multiple_of(g * w, w) for w in (gw, nn, per))
@@ -155,61 +200,92 @@
         ex = exact(jnp.exp(cl - cum), spread, TN)
         e_x[:, cols] = ex
         hrows = pl.ds(at, gw)
-        dec_x[hrows, :] = exact(spread, jnp.broadcast_to(jnp.exp(cl), (per, nn)), TN)
+        dec_x[hrows, :] = exact(spread, decs[rows, :], TN)
         summ[hrows, :] = dot3(split(s * sx * ex), split(bv), TN)
+        for i in range(half):
+            summary_copy(theirs(g * half + i)).start()
         return 0
 
     lax.fori_loop(0, groups, local, 0)
 
-    @pl.when(first)
-    def _():
-        ent[...] = state_ref[...]
-
-    def piece(k):
-        return pl.ds(pl.multiple_of(k * bw, bw), bw)
-
-    def forward_copy(k):
-        return remote(exi.at[piece(k), :], ent.at[piece(k), :], fs_sem.at[k], fr_sem.at[k], after)
-
-    def forward(k, _):
-        @pl.when(jnp.logical_not(first))
+    dec_copy.wait_recv()
+
+    def spread_decay(g, _):
+        rows = pl.ds(pl.multiple_of(g * per, per), per)
+        pdec_x[pl.ds(pl.multiple_of(g * gw, gw), gw), :] = exact(spread, pdecs[rows, :], TN)
+        return 0
+
+    lax.fori_loop(0, groups, spread_decay, 0)
+
+    @pl.when(first_pair)
+    def _():
+        ebuf[...] = state_ref[...]
+
+    @pl.when(last_pair)
+    def _():
+        gbuf[...] = jnp.zeros_like(gbuf)
+
+    def ordered(here, there):
+        return jnp.where(left, here, there), jnp.where(left, there, here)
+
+    def forward(m, _):
+        k = mine(m)
+        rows = piece(k)
+        summary_copy(k).wait_recv()
+
+        @pl.when(jnp.logical_not(first_pair))
         def _():
             forward_copy(k).wait_recv()
 
+        decay_a, decay_b = ordered(dec_x[rows, :], pdec_x[rows, :])
+        sum_a, sum_b = ordered(summ[rows, :], psum[rows, :])
+        enter = ebuf[rows, :]
+        middle = decay_a * enter + sum_a
+
+        @pl.when(jnp.logical_not(last_pair))
+        def _():
+            f_out[rows, :] = decay_b * middle + sum_b
+            forward_copy(k).start()
+
+        ent[rows, :], f_other[rows, :] = ordered(enter, middle)
+        enter_copy(k).start()
+        return 0
+
+    def backward(m, _):
+        k = mine(m)
         rows = piece(k)
-        exi[rows, :] = dec_x[rows, :] * ent[rows, :] + summ[rows, :]
-
-        @pl.when(jnp.logical_not(last))
-        def _():
-            forward_copy(k).start()
-
-        return 0
-
-    lax.fori_loop(0, chunks, forward, 0)
-
-    def backward_copy(k):
-        return remote(back.at[piece(k), :], d_exi.at[piece(k), :], bs_sem.at[k], br_sem.at[k], before)
-
-    def backward(k, _):
-        @pl.when(jnp.logical_not(last))
+        grad_out_copy(k).wait_recv()
+
+        @pl.when(jnp.logical_not(last_pair))
         def _():
             backward_copy(k).wait_recv()
 
-        @pl.when(jnp.logical_not(first))
-        def _():
-            rows = piece(k)
-            back[rows, :] = dec_x[rows, :] * d_exi[rows, :] + d_ent[rows, :]
+        decay_a, decay_b = ordered(dec_x[rows, :], pdec_x[rows, :])
+        grad_a, grad_b = ordered(d_ent[rows, :], pd_ent[rows, :])
+        leave = gbuf[rows, :]
+        middle = decay_b * leave + grad_b
+
+        @pl.when(jnp.logical_not(first_pair))
+        def _():
+            b_out[rows, :] = decay_a * middle + grad_a
             backward_copy(k).start()
 
-        return 0
-
-    @pl.when(last)
-    def _():
-        d_exi[...] = jnp.zeros_like(d_exi)
+        d_exi[rows, :], b_other[rows, :] = ordered(middle, leave)
+        exit_copy(k).start()
+        return 0
+
+    lax.fori_loop(0, jnp.where(last_pair, half, own), forward, 0)
 
     def output(g, _):
         at, nat, hat = (pl.multiple_of(g * w, w) for w in (gw, nn, per))
         cols, ncols, rows = pl.ds(at, gw), pl.ds(nat, nn), pl.ds(hat, per)
+
+        @pl.when(last_pair & (g < groups - 1))
+        def _():
+            lax.fori_loop((g + 1) * half, (g + 2) * half, forward, 0)
+
+        for i in range(half):
+            enter_copy(theirs(g * half + i)).wait_recv()
         bs, cs = split(bco[:, ncols]), split(cco[:, ncols])
         scores = dot3(cs, bs, NT)
         scores_t = dot3(bs, cs, NT)
@@ -248,10 +324,12 @@
         r1_s[rows, :] = sum(dot(spread_b, v, NT) for v in split(dm * inner))
         dcar = split(dm * ecum_x[:, cols])
         d_ent[pl.ds(at, gw), :] = dot3(dcar, cs, TN)
-
-        @pl.when(last)
-        def _():
-            lax.fori_loop(g * blocks, (g + 1) * blocks, backward, 0)
+        for i in range(half):
+            grad_out_copy(theirs(g * half + i)).start()
+
+        @pl.when(last_pair & (g > 0))
+        def _():
+            lax.fori_loop((g - 1) * half, g * half, backward, 0)
 
         ds = jnp.zeros((tok, tok), F32)
         for j in range(blocks):
@@ -274,6 +352,9 @@
 
     lax.fori_loop(0, groups, output, 0)
 
+    lax.fori_loop(
+        jnp.where(last_pair, own - half, 0), jnp.where(first_pair, half, own), backward, 0
+    )
     from_t = (iota((tok, tok), 0) >= iota((tok, tok), 1)).astype(F32)
 
     def grad_copy(g):
@@ -287,9 +368,12 @@
         at, nat, hat = (pl.multiple_of(g * w, w) for w in (gw, nn, per))
         cols, ncols, rows = pl.ds(at, gw), pl.ds(nat, nn), pl.ds(hat, per)
 
-        @pl.when(jnp.logical_not(last))
-        def _():
-            lax.fori_loop(g * blocks, (g + 1) * blocks, backward, 0)
+        @pl.when(first_pair & (g < groups - 1))
+        def _():
+            lax.fori_loop((g + 1) * half, (g + 2) * half, backward, 0)
+
+        for i in range(half):
+            exit_copy(theirs(g * half + i)).wait_recv()
 
         grad = d_exi[pl.ds(at, gw), :]
         grads = split(grad)
@@ -313,7 +397,9 @@
             grad_copy(g).start()
 
         u = sum(dot(spread_b, v, NT) for v in split(s * both))
-        lane = jnp.sum(exact(spread, grad * exi[pl.ds(at, gw), :]), axis=1, keepdims=True)
+        hrows = pl.ds(at, gw)
+        leave = dec_x[hrows, :] * ent[hrows, :] + summ[hrows, :]
+        lane = jnp.sum(exact(spread, grad * leave), axis=1, keepdims=True)
         st = step_row[rows, :]
         d_rate = exact(r1_s[rows, :] - st * u, from_t) + lane
         gdt_ref[rows, :] = (u - acol[rows, :] * d_rate) * sigmoid(dt_ref[rows, :])
@@ -348,25 +434,33 @@
 
     lax.fori_loop(0, groups, finish, 0)
 
+    dec_copy.wait_send()
+
+    def drain(m, _):
+        summary_copy(theirs(m)).wait_send()
+        grad_out_copy(theirs(m)).wait_send()
+        enter_copy(mine(m)).wait_send()
+        exit_copy(mine(m)).wait_send()
+
+        @pl.when(jnp.logical_not(last_pair))
+        def _():
+            forward_copy(mine(m)).wait_send()
+
+        @pl.when(jnp.logical_not(first_pair))
+        def _():
+            backward_copy(mine(m)).wait_send()
+
+        return 0
+
+    lax.fori_loop(0, own, drain, 0)
+
     @pl.when(jnp.logical_not(last))
     def _():
         for copy in halos:
             copy.wait_send()
 
-        def drain(k, _):
-            forward_copy(k).wait_send()
-            return 0
-
-        lax.fori_loop(0, chunks, drain, 0)
-
     @pl.when(jnp.logical_not(first))
     def _():
-        def drain(k, _):
-            backward_copy(k).wait_send()
-            return 0
-
-        lax.fori_loop(0, chunks, drain, 0)
-
         def drain_halo(g, _):
             grad_copy(g).wait_send()
             return 0
@@ -392,12 +486,11 @@
         v(16, chan, dtype=BF16), v(16, wide, dtype=BF16), v(16, wide, dtype=BF16),
         v(tok + 8, gw), v(tok, chan), v(tok, wide), v(tok, wide), v(tok, chan), v(tok, wide), v(tok, wide),
         v(heads, tok), v(heads, tok), v(heads, 128), v(heads, 128), v(groups, tok, 128),
-        v(tok, chan), v(tok, chan), v(tok, chan), v(chan, nn),
-        v(chan, nn), v(chan, nn), v(chan, nn), v(chan, nn), v(chan, nn), v(chan, nn),
+        v(tok, chan), v(tok, chan), v(tok, chan), v(chan, nn), v(chan, nn), v(heads, 128), v(heads, 128),
+        *([v(chan, nn)] * 12),
         v(tok, chan), v(heads, tok), v(tok, chan), v(tok, wide), v(tok, wide), v(per, tok, tok),
         v(tok + 8, chan), v(groups, 8, gw + 2 * nn), v(groups, 8, gw + 2 * nn), v(groups, tok + 8, 2 * nn),
-        dma((3,)), dma((3,)), dma((chunks,)), dma((chunks,)), dma((chunks,)), dma((chunks,)),
-        dma((groups,)), dma((groups,)),
+        dma((4,)), dma((4,)), dma((6, 2, chunks)), dma((groups,)), dma((groups,)),
     ]
     vmem = pl.BlockSpec(memory_space=pltpu.VMEM)
     outs = [

time: 119 us -> 84.7 us (0.71)
  Pallas kernels: 113 us -> 78.5 us
    pallas_call x1, Pallas kernels: 113 us -> 78.5 us  [per_device(): pl.pallas_call(kernel, out_shape=outs, in_specs=[vmem] * 13, out_specs=[v...]
where the time goes in v2:
time: 84.7 us; the launch traced here: 84.4 us
  Pallas kernels  78.5 us (93%)
  local copies, waits for them, and re-layouts  5.29 us (6%)
    pallas_call x1, Pallas kernels, per_device(): pl.pallas_call(kernel, out_shape=outs, in_specs=[vmem] * 13, out_specs=[v...  78.5 us
    unnamed x13, local copies, waits for them, and re-layouts  5.29 us

profile of v2, /device:TPU:0, one launch (start us, length us, event | category | flops | bytes accessed | tf_op | source)
XLA Modules:
  0.0 84.4 jit_solution(13210534792098135825)
XLA Ops:
  0.6 78.5 %shard_map.164 = (bf16[128,2048]{1,0:T(8,128)(2,1)}, bf16[128,2048]{1,0:T(8,128)(2,1)}, bf16[128,512]{1,0:T(8,128)(2,1)}, bf16[128,512]{1,0:T(8,128)(2,1)}, f32[64,128]{1,0:T(8,128)}) custom-call(bf16[128,2048]{1,0:T(8,128)(2,1)} %x_ref.1, bf16[128,2048]{1,0:T(8,128)(2,1)} %z_ref.1, bf16[128,512]{1,0:T(8,128)(2,1)} %b_ref.1, bf16[128,512]{1,0:T(8,128)(2,1)} %c_ref.1, ...), custom_call_target="tpu_custom_call" | custom-call | tf_op jit(solution)/shard_map/pallas_call | solution.py:499
  79.1 0.0 copy-start
  79.1 1.9 %copy.23 = bf16[128,2048]{1,0:T(8,128)(2,1)} copy(bf16[128,2048]{1,0:T(8,128)(2,1)} %get-tuple-element.10) | data formatting | bytes 1048576
  81.1 0.0 copy-done
  81.1 0.0 copy-start.2
  81.1 0.8 copy.24
  81.9 0.2 copy-done.2
  82.1 0.0 copy-start.1
  82.1 0.7 copy.25
  82.7 0.3 copy-done.1
  83.0 0.0 copy-start.3
  83.0 0.7 copy.26
  83.7 0.1 copy-done.3
  83.8 0.6 copy.27
Async XLA Ops:
  79.1 2.0 %copy-start = (bf16[128,2048]{1,0:T(8,128)(2,1)S(1)}, bf16[128,2048]{1,0:T(8,128)(2,1)}, u32[]{:S(2)}) copy-start(bf16[128,2048]{1,0:T(8,128)(2,1)} %get-tuple-element.11) | copy-start | bytes 1572868
  81.1 1.0 %copy-start.2 = (bf16[128,512]{1,0:T(8,128)(2,1)S(1)}, bf16[128,512]{1,0:T(8,128)(2,1)}, u32[]{:S(2)}) copy-start(bf16[128,512]{1,0:T(8,128)(2,1)} %get-tuple-element.12) | copy-start | bytes 393220
  82.1 1.0 %copy-start.1 = (bf16[128,512]{1,0:T(8,128)(2,1)S(1)}, bf16[128,512]{1,0:T(8,128)(2,1)}, u32[]{:S(2)}) copy-start(bf16[128,512]{1,0:T(8,128)(2,1)} %get-tuple-element.13) | copy-start | bytes 393220
  83.0 0.8 copy-start.3

commit v3 on v2

--- a/solution.py
+++ b/solution.py
@@ -13,6 +13,7 @@
 F32, BF16 = jnp.float32, jnp.bfloat16
 NN, NT, TN = (((1,), (0,)), ((1,), (1,)), ((0,), (0,)))
 BLOCK = 4
+PIECE = 4
 
 
 def split(a):
@@ -62,7 +63,9 @@
     bw = BLOCK * hd
     blocks = gw // bw
     taps = wx_ref.shape[0]
-    half = blocks // 2
+    cw = PIECE * hd
+    pieces = gw // cw
+    half = pieces // 2
     own = groups * half
     side, pair, pairs = lax.rem(me, 2), me // 2, peers // 2
     first_pair, last_pair = pair == 0, pair == pairs - 1
@@ -146,7 +149,7 @@
         return total
 
     def piece(k):
-        return pl.ds(pl.multiple_of(k * bw, bw), bw)
+        return pl.ds(pl.multiple_of(k * cw, cw), cw)
 
     def moved(way, src, dst, k, to):
         return remote(
@@ -154,10 +157,10 @@
         )
 
     def mine(m):
-        return m // half * blocks + side * half + lax.rem(m, half)
+        return m // half * pieces + side * half + lax.rem(m, half)
 
     def theirs(m):
-        return m // half * blocks + (1 - side) * half + lax.rem(m, half)
+        return m // half * pieces + (1 - side) * half + lax.rem(m, half)
 
     def summary_copy(k):
         return moved(0, summ, psum, k, partner)
@@ -468,6 +471,12 @@
         lax.fori_loop(0, groups, drain_halo, 0)
 
 
+def write_out(*refs):
+    count = len(refs) // 2
+    for src, dst in zip(refs[:count], refs[count:]):
+        dst[...] = src[...]
+
+
 def per_device(
     x_stream, z_stream, b_stream, c_stream, dt_raw, a_log, skip_coef, conv_x, conv_b, conv_c, norm_gain, state_in, grad_out
 ):
@@ -476,7 +485,7 @@
     wide = b_stream.shape[1]
     groups = wide // nn
     per, gw = heads // groups, chan // groups
-    chunks = chan // (BLOCK * hd)
+    chunks = chan // (PIECE * hd)
     dma = pltpu.SemaphoreType.DMA
 
     def v(*shape, dtype=F32):
@@ -496,7 +505,7 @@
     outs = [
         jax.ShapeDtypeStruct(a.shape, a.dtype) for a in (x_stream, z_stream, b_stream, c_stream, dt_raw)
     ]
-    return pl.pallas_call(
+    results = pl.pallas_call(
         kernel,
         out_shape=outs,
         in_specs=[vmem] * 13,
@@ -509,6 +518,7 @@
         x_stream, z_stream, b_stream, c_stream, dt_raw, a_log.reshape(1, heads), skip_coef.reshape(1, heads),
         conv_x, conv_b, conv_c, norm_gain.reshape(1, chan), state_in.reshape(heads * hd, nn), grad_out,
     )
+    return pl.pallas_call(write_out, out_shape=outs, in_specs=[vmem] * 5, out_specs=[vmem] * 5)(*results)
 
 
 def solution(mesh):

time: 84.7 us -> 81.6 us (0.963)
  local copies, waits for them, and re-layouts: 5.29 us -> 0 us
  Pallas kernels: 78.5 us -> 80.8 us
    unnamed x13 -> x0, local copies, waits for them, and re-layouts: 5.29 us -> none
    pallas_call x0 -> x1, Pallas kernels: none -> 2.34 us  [per_device(): pl.pallas_call(write_out, out_shape=outs, in_specs=[vmem] * 5, out_specs=...]
where the time goes in v3:
time: 81.6 us; the launch traced here: 81.4 us
  Pallas kernels  80.8 us (99%)
    pallas_call x1, Pallas kernels, per_device(): pl.pallas_call(kernel, out_shape=outs, in_specs=[vmem] * 13, out_specs=[v...  78.4 us
    pallas_call x1, Pallas kernels, per_device(): pl.pallas_call(write_out, out_shape=outs, in_specs=[vmem] * 5, out_specs=...  2.34 us

profile of v3, /device:TPU:0, one launch (start us, length us, event | category | flops | bytes accessed | tf_op | source)
XLA Modules:
  0.0 81.4 jit_solution(8175534021481048221)
XLA Ops:
  0.6 78.4 %shard_map.164 = (bf16[128,2048]{1,0:T(8,128)(2,1)}, bf16[128,2048]{1,0:T(8,128)(2,1)}, bf16[128,512]{1,0:T(8,128)(2,1)}, bf16[128,512]{1,0:T(8,128)(2,1)}, f32[64,128]{1,0:T(8,128)}) custom-call(bf16[128,2048]{1,0:T(8,128)(2,1)} %x_ref.1, bf16[128,2048]{1,0:T(8,128)(2,1)} %z_ref.1, bf16[128,512]{1,0:T(8,128)(2,1)} %b_ref.1, bf16[128,512]{1,0:T(8,128)(2,1)} %c_ref.1, ...), custom_call_target="tpu_custom_call" | custom-call | tf_op jit(solution)/shard_map/pallas_call | solution.py:508
  79.1 2.3 %shard_map.165 = (bf16[128,2048]{1,0:T(8,128)(2,1)}, bf16[128,2048]{1,0:T(8,128)(2,1)}, bf16[128,512]{1,0:T(8,128)(2,1)}, bf16[128,512]{1,0:T(8,128)(2,1)}, f32[64,128]{1,0:T(8,128)}) custom-call(bf16[128,2048]{1,0:T(8,128)(2,1)} %get-tuple-element.10.refs_0_, bf16[128,2048]{1,0:T(8,128)(2,1)} %get-tuple-element.11.refs_1_, ...), custom_call_target="tpu_custom_call" | custom-call | tf_op jit(solution)/shard_map/pallas_call | solution.py:521

commit v4 on v3

--- a/solution.py
+++ b/solution.py
@@ -191,15 +191,11 @@
         pre_b[:, ncols] = pb
         bv = pb * sigmoid(pb)
         bco[:, ncols] = bv
-        pc = conv(c_ref, halo_c, wc_ref, nat, nn)
-        pre_c[:, ncols] = pc
-        cco[:, ncols] = pc * sigmoid(pc)
         cum, st = cum_row[rows, :], step_row[rows, :]
         cl = cum[:, tok - 1 : tok]
         cum_t[g] = jnp.concatenate([cum, jnp.zeros((128 - per, tok), F32)], axis=0).T
         sx = exact(st, spread, TN)
         step_x[:, cols] = sx
-        ecum_x[:, cols] = exact(jnp.exp(cum), spread, TN)
         ex = exact(jnp.exp(cl - cum), spread, TN)
         e_x[:, cols] = ex
         hrows = pl.ds(at, gw)
@@ -207,6 +203,10 @@
         summ[hrows, :] = dot3(split(s * sx * ex), split(bv), TN)
         for i in range(half):
             summary_copy(theirs(g * half + i)).start()
+        pc = conv(c_ref, halo_c, wc_ref, nat, nn)
+        pre_c[:, ncols] = pc
+        cco[:, ncols] = pc * sigmoid(pc)
+        ecum_x[:, cols] = exact(jnp.exp(cum), spread, TN)
         return 0
 
     lax.fori_loop(0, groups, local, 0)

time: 81.6 us -> 81.3 us (level)
  no operation moved by 1% of the time
where the time goes in v4:
time: 81.3 us; the launch traced here: 81.1 us
  Pallas kernels  80.5 us (99%)
    pallas_call x1, Pallas kernels, per_device(): pl.pallas_call(kernel, out_shape=outs, in_specs=[vmem] * 13, out_specs=[v...  78.2 us
    pallas_call x1, Pallas kernels, per_device(): pl.pallas_call(write_out, out_shape=outs, in_specs=[vmem] * 5, out_specs=...  2.34 us

profile of v4, /device:TPU:0, one launch (start us, length us, event | category | flops | bytes accessed | tf_op | source)
XLA Modules:
  0.0 81.1 jit_solution(18035759569240792621)
XLA Ops:
  0.6 78.2 %shard_map.164 = (bf16[128,2048]{1,0:T(8,128)(2,1)}, bf16[128,2048]{1,0:T(8,128)(2,1)}, bf16[128,512]{1,0:T(8,128)(2,1)}, bf16[128,512]{1,0:T(8,128)(2,1)}, f32[64,128]{1,0:T(8,128)}) custom-call(bf16[128,2048]{1,0:T(8,128)(2,1)} %x_ref.1, bf16[128,2048]{1,0:T(8,128)(2,1)} %z_ref.1, bf16[128,512]{1,0:T(8,128)(2,1)} %b_ref.1, bf16[128,512]{1,0:T(8,128)(2,1)} %c_ref.1, ...), custom_call_target="tpu_custom_call" | custom-call | tf_op jit(solution)/shard_map/pallas_call | solution.py:508
  78.8 2.3 %shard_map.165 = (bf16[128,2048]{1,0:T(8,128)(2,1)}, bf16[128,2048]{1,0:T(8,128)(2,1)}, bf16[128,512]{1,0:T(8,128)(2,1)}, bf16[128,512]{1,0:T(8,128)(2,1)}, f32[64,128]{1,0:T(8,128)}) custom-call(bf16[128,2048]{1,0:T(8,128)(2,1)} %get-tuple-element.10.refs_0_, bf16[128,2048]{1,0:T(8,128)(2,1)} %get-tuple-element.11.refs_1_, ...), custom_call_target="tpu_custom_call" | custom-call | tf_op jit(solution)/shard_map/pallas_call | solution.py:521
